TPU v7x, 256 devices: a whole 4x4x8 slice. The times are simulated.
256 devices in a mesh: dp: 128 (over z, x, y), pair: 2 (over core).
Axes of the slice: x: 4, y: 4, z: 8, core: 2. Of those that a mesh axis runs over, the one named last changes fastest.
Arguments:
- hidden_in: bfloat16 [32768, 1536], P(('dp', 'pair')), may hold values from -24 to 24
- segment_ids: int32 [32768], replicated, may hold values from 0 to 511, as said below
- frame_mask: int32 [32768], P(('dp', 'pair')), may hold values from 0 to 1, as said below
- dw_kernel: float32 [31, 1536], P(None, ('dp', 'pair')), may hold values from -1 to 1
- norm_scale: float32 [1536], P(('dp', 'pair')), may hold values from 0.1 to 1.9
- norm_shift: float32 [1536], P(('dp', 'pair')), may hold values from -3 to 3
- out_weight: bfloat16 [1536, 1536], P(('dp', 'pair')), may hold values from -0.15625 to 0.15625
- cotangent: bfloat16 [32768, 1536], P(('dp', 'pair')), may hold values from -6 to 6
Outputs:
- module_out: bfloat16 [32768, 1536], P(('dp', 'pair'))
- grad_hidden: bfloat16 [32768, 1536], P(('dp', 'pair'))
- grad_kernel: float32 [31, 1536], P(None, ('dp', 'pair'))
- grad_scale: float32 [1536], P(('dp', 'pair'))
- grad_shift: float32 [1536], P(('dp', 'pair'))
- grad_weight: float32 [1536, 1536], P(('dp', 'pair'))
Inputs may be any that keep to these rules, and one draw needn't show every extreme that they name: `segment_ids`: non-falling along the stream, starting at 0; each utterance has 1 to 192 frames; no utterance begins at a frame whose index is a positive multiple of 128. `frame_mask`: 1 on every frame whose index modulo 16 is 0 or 15.
All inputs are finite; a program needn't handle non-finite values.
Results may differ from a plain program's by a relative error of at most 0.0049.
Values may be sent and summed in bfloat16 or wider, within the bound.
No kernel may reach another device: no remote copies, remote signals or barrier semaphores. Data moves between devices by JAX's collectives and lax.ppermute only.
A program may use at most 128 MiB of HBM per device.

v0:
```python
import jax
import jax.numpy as jnp
from jax import lax
from jax.sharding import PartitionSpec as P

KERNEL = 31


def padded(cells, sides, width):
    for axis, dim in sides:
        count = lax.axis_size(axis)
        ends = count - 1
        head = lax.slice_in_dim(cells, 0, width, axis=dim)
        tail = lax.slice_in_dim(cells, cells.shape[dim] - width, cells.shape[dim], axis=dim)
        cells = jnp.concatenate(
            [
                lax.ppermute(tail, axis, [(i, (i + 1) % count) for i in range(ends)]),
                cells,
                lax.ppermute(head, axis, [((i + 1) % count, i) for i in range(ends)]),
            ],
            axis=dim,
        )
    return cells


def local(
    hidden_in, segment_ids, frame_mask, dw_kernel, norm_scale, norm_shift, out_weight, cotangent
):
    local_rows = hidden_in.shape[0]
    shard_cols = norm_scale.shape[0]
    half = KERNEL // 2
    device_pos = lax.axis_index(("dp", "pair"))
    weight_col = frame_mask.astype(jnp.float32)[:, None]
    stacked = jnp.concatenate([dw_kernel, norm_scale[None, :], norm_shift[None, :]], axis=0)
    params_full = lax.all_gather(stacked, ("dp", "pair"), axis=1, tiled=True)
    kernel_full = params_full[:KERNEL]
    scale_full = params_full[KERNEL]
    shift_full = params_full[KERNEL + 1]
    seg_pad = jnp.pad(segment_ids, (half, half), constant_values=-1)
    seg_local = lax.dynamic_slice_in_dim(seg_pad, device_pos * local_rows, local_rows + 2 * half)
    own_seg = seg_local[half : half + local_rows]
    masked = jnp.where(frame_mask[:, None] == 1, hidden_in, jnp.zeros_like(hidden_in))
    padded_in = padded(masked, ((("dp", "pair"), 0),), half).astype(jnp.float32)
    conv = jnp.zeros((local_rows, params_full.shape[1]), jnp.float32)
    for offset in range(KERNEL):
        same_seg = (seg_local[offset : offset + local_rows] == own_seg)[:, None]
        conv = conv + jnp.where(
            same_seg, kernel_full[offset] * padded_in[offset : offset + local_rows], 0.0
        )
    total, count = lax.psum(
        (jnp.sum(weight_col * conv, axis=0), jnp.sum(weight_col)), ("dp", "pair")
    )
    mean = total / count
    centred = conv - mean
    spread = lax.psum(jnp.sum(weight_col * centred * centred, axis=0), ("dp", "pair"))
    variance = spread / count
    inv_std = lax.rsqrt(variance + 1e-05)
    normed = centred * inv_std
    pre = scale_full * normed + shift_full
    sig = jax.nn.sigmoid(pre)
    act = (weight_col * pre * sig).astype(jnp.bfloat16)
    weight_full = lax.all_gather(out_weight, ("dp", "pair"), axis=0, tiled=True)
    module_out = jnp.dot(act, weight_full, preferred_element_type=jnp.float32).astype(jnp.bfloat16)
    grad_act = lax.dot_general(
        cotangent, weight_full, (((1,), (1,)), ((), ())), preferred_element_type=jnp.float32
    )
    grad_pre = weight_col * grad_act * sig * (1.0 + pre * (1.0 - sig))
    scale_sum, shift_sum = lax.psum(
        (jnp.sum(grad_pre * normed, axis=0), jnp.sum(grad_pre, axis=0)), ("dp", "pair")
    )
    col_start = device_pos * shard_cols
    grad_scale = lax.dynamic_slice_in_dim(scale_sum, col_start, shard_cols)
    grad_shift = lax.dynamic_slice_in_dim(shift_sum, col_start, shard_cols)
    grad_conv = (
        weight_col
        * scale_full
        * inv_std
        * (grad_pre - shift_sum / count - normed * scale_sum / count)
    )
    grad_pad = padded(grad_conv, ((("dp", "pair"), 0),), half)
    grad_local = jnp.zeros_like(grad_conv)
    tap_rows = []
    for offset in range(KERNEL):
        same_fwd = (seg_local[offset : offset + local_rows] == own_seg)[:, None]
        tap_rows.append(
            jnp.sum(
                jnp.where(same_fwd, grad_conv * padded_in[offset : offset + local_rows], 0.0),
                axis=0,
            )
        )
        back = 2 * half - offset
        same_back = (seg_local[back : back + local_rows] == own_seg)[:, None]
        grad_local = grad_local + jnp.where(
            same_back, kernel_full[offset] * grad_pad[back : back + local_rows], 0.0
        )
    grad_kernel = lax.psum_scatter(
        jnp.stack(tap_rows, axis=0), ("dp", "pair"), scatter_dimension=1, tiled=True
    )
    grad_hidden = (weight_col * grad_local).astype(jnp.bfloat16)
    grad_weight = lax.psum_scatter(
        lax.dot_general(
            act, cotangent, (((0,), (0,)), ((), ())), preferred_element_type=jnp.float32
        ),
        ("dp", "pair"),
        scatter_dimension=0,
        tiled=True,
    )
    return (module_out, grad_hidden, grad_kernel, grad_scale, grad_shift, grad_weight)


def solution(mesh):
    return jax.shard_map(
        local,
        mesh=mesh,
        in_specs=(
            P(("dp", "pair"), None),
            P(),
            P(("dp", "pair")),
            P(None, ("dp", "pair")),
            P(("dp", "pair")),
            P(("dp", "pair")),
            P(("dp", "pair"), None),
            P(("dp", "pair"), None),
        ),
        out_specs=(
            P(("dp", "pair"), None),
            P(("dp", "pair"), None),
            P(None, ("dp", "pair")),
            P(("dp", "pair")),
            P(("dp", "pair")),
            P(("dp", "pair"), None),
        ),
        check_vma=False,
    )
```

profile of v0, /device:TPU:1, one launch (start us, length us, event | category | flops | bytes accessed | tf_op | source)
XLA Modules:
  0.0 1933.7 jit_solution(4667449494425731221)
XLA Ops:
  9.7 4.6 collective-permute-start
  19.3 68.0 %all-gather = f32[256,6,33]{2,1,0:T(8,128)S(1)} all-gather(f32[1,6,33]{2,1,0:T(8,128)S(1)} %maximum_bitcast_fusion), channel_id=1, replica_groups=mesh['dp'=128,'pair'=2] {'dp','pair'}, dimensions={0}, use_global_device_ids=true | all-gather | bytes 203544 | tf_op jit(solution)/shard_map/all_gather | solution.py:35
  88.0 5.6 slice_reduce_fusion.31
  93.6 8.2 slice_reduce_fusion.32
  102.8 4.6 multiply_reduce_fusion.2
  107.4 75.7 %all-reduce.5 = (f32[1536]{0:T(1024)S(1)}, f32[]{:T(128)}) all-reduce(f32[1536]{0:T(1024)S(1)} %get-tuple-element.89, f32[]{:T(128)} %convert_reduce_fusion), channel_id=1, replica_groups=mesh['dp'=128,'pair'=2] {'dp','pair'}, use_global_device_ids=true, to_apply=%region_1.2 | all-reduce | flops 1537 | bytes 12296 | tf_op jit(solution)/shard_map/psum | solution.py:50
  184.0 74.2 %psum.37 = f32[1536]{0:T(1024)S(1)} all-reduce(f32[1536]{0:T(1024)S(1)} %fusion.119), channel_id=1, replica_groups=mesh['dp'=128,'pair'=2] {'dp','pair'}, use_global_device_ids=true, to_apply=%region_5.6 | all-reduce | flops 1536 | bytes 12288 | tf_op jit(solution)/shard_map/psum | solution.py:55
  258.9 5.2 fusion.124
  264.0 709.9 %fusion = f32[8,1536]{1,0:T(8,128)S(1)} fusion(f32[1536,1536]{1,0:T(8,128)} %fusion.124), kind=kCustom, calls=%all-reduce-scatter | all-reduce-scatter fusion | flops 3145729 | bytes 9486336
  978.8 11.0 collective-permute-start.67
  1005.7 17.9 collective-permute-start.51
  1060.5 6.1 collective-permute-start.35
  1066.6 13.1 collective-permute-start.34
  1079.7 13.1 collective-permute-start.33
  1092.9 13.1 collective-permute-start.32
  1106.0 13.1 collective-permute-start.31
  1119.2 13.1 collective-permute-start.30
  1132.3 13.1 collective-permute-start.29
  1145.5 13.1 collective-permute-start.28
  1158.6 13.1 collective-permute-start.27
  1171.8 13.1 collective-permute-start.26
  1184.9 13.1 collective-permute-start.25
  1198.1 13.1 collective-permute-start.24
  1211.2 13.1 collective-permute-start.23
  1224.4 13.1 collective-permute-start.22
  1237.5 13.1 collective-permute-start.21
  1250.7 13.1 collective-permute-start.20
  1263.8 13.1 collective-permute-start.19
  1277.0 13.1 collective-permute-start.18
  1290.1 13.1 collective-permute-start.17
  1303.3 13.1 collective-permute-start.16
  1316.4 13.3 collective-permute-start.15
  1329.7 13.1 collective-permute-start.14
  1342.9 13.1 collective-permute-start.13
  1356.0 13.1 collective-permute-start.12
  1369.2 13.1 collective-permute-start.11
  1382.3 13.1 collective-permute-start.10
  1395.5 13.1 collective-permute-start.9
  1408.6 13.7 collective-permute-start.8
  1422.4 13.1 collective-permute-start.7
  1435.5 13.1 collective-permute-start.6
  1448.7 13.1 collective-permute-start.5
  1466.0 97.2 %concatenate.45 = f32[518,1536]{1,0:T(8,128)} concatenate(f32[6,1536]{1,0:T(8,128)S(1)} %collective-permute-done.67, f32[8,1536]{1,0:T(8,128)S(1)} %collective-permute-done.66, f32[8,1536]{1,0:T(8,128)S(1)} %collective-permute-done.65, f32[8,1536]{1,0:T(8,128)S(1)} %collective-permute-done.64, f32[8,1536]{1,0:T(8,128)S(1)} %collective-permute-done.63, ...), dimensions={0} | concatenate | bytes 6365184
  1564.7 8.4 reshape.52
  1573.1 4.1 convolution_convert_fusion
  1580.0 79.5 %all-reduce.4 = (f32[1536]{0:T(1024)S(1)}, f32[1536]{0:T(1024)S(1)}) all-reduce(f32[1536]{0:T(1024)S(1)} %get-tuple-element.50, f32[1536]{0:T(1024)S(1)} %get-tuple-element.49), channel_id=1, replica_groups=mesh['dp'=128,'pair'=2] {'dp','pair'}, use_global_device_ids=true, to_apply=%region_9.10 | all-reduce | flops 3072 | bytes 24576 | tf_op jit(solution)/shard_map/psum | solution.py:68
  1678.1 9.9 fusion.9
  1688.0 237.1 %all-reduce.8.cloned.1.call-done = f32[31,1536]{1,0:T(8,128)} async-done(((f32[31,1536]{1,0:T(8,128)}), f32[31,1536]{1,0:T(8,128)}) %all-reduce.8.cloned.1.call-update) | async-done | bytes 190480
  (346 shorter events, 94.8 us)
Async XLA Ops:
  7.2 1557.6 %all-gather.4.cloned.1.call-start = ((), (), s32[]{:S(2)}) async-start(), calls=%async_computation | async-start | bytes 6316032 | tf_op jit(solution)/shard_map/all_gather | solution.py:62
  7.9 1917.2 %all-reduce.8.cloned.1.call-start = ((), (), s32[]{:S(2)}) async-start(), calls=%async_computation.1 | async-start | bytes 393216
  9.7 92.7 %collective-permute-start = (bf16[15,1536]{1,0:T(8,128)(2,1)S(1)}, bf16[15,1536]{1,0:T(8,128)(2,1)S(1)}, u32[]{:S(2)}, u32[]{:S(2)}) collective-permute-start(bf16[15,1536]{1,0:T(8,128)(2,1)S(1)} %get-tuple-element.93), channel_id=1, source_target_pairs={{0,1},{1,2},{2,3},{3,4},{4,5},{5,6},{6,7},{7,8},{8,9},{9,10},{10,1... | collective-permute-start | bytes 138248 | tf_op jit(solution)/shard_map/ppermute | solution.py:17
  14.3 88.1 %collective-permute-start.1 = (bf16[15,1536]{1,0:T(8,128)(2,1)S(1)}, bf16[15,1536]{1,0:T(8,128)(2,1)S(1)}, u32[]{:S(2)}, u32[]{:S(2)}) collective-permute-start(bf16[15,1536]{1,0:T(8,128)(2,1)S(1)} %get-tuple-element.94), channel_id=1, source_target_pairs={{1,0},{2,1},{3,2},{4,3},{5,4},{6,5},{7,6},{8,7},{9,8},{10,9},{11,1... | collective-permute-start | bytes 138248 | tf_op jit(solution)/shard_map/ppermute | solution.py:19
  974.0 18.7 collective-permute-start.66
  975.3 18.7 collective-permute-start.65
  977.5 17.8 collective-permute-start.64
  1000.5 23.2 %collective-permute-start.55 = (f32[8,1536]{1,0:T(8,128)S(1)}, f32[8,1536]{1,0:T(8,128)S(1)}, u32[]{:S(2)}, u32[]{:S(2)}) collective-permute-start(f32[8,1536]{1,0:T(8,128)S(1)} %fusion), channel_id=1, source_target_pairs={{0,52},{1,53},{2,54},{3,55},{4,56},{5,57},{6,58},{7,59},{8,60},{9,... | collective-permute-start | bytes 147464
  1001.8 25.0 %collective-permute-start.54 = (f32[8,1536]{1,0:T(8,128)S(1)}, f32[8,1536]{1,0:T(8,128)S(1)}, u32[]{:S(2)}, u32[]{:S(2)}) collective-permute-start(f32[8,1536]{1,0:T(8,128)S(1)} %fusion), channel_id=1, source_target_pairs={{0,51},{1,52},{2,53},{3,54},{4,55},{5,56},{6,57},{7,58},{8,59},{9,... | collective-permute-start | bytes 147464
  1003.1 25.3 %collective-permute-start.53 = (f32[8,1536]{1,0:T(8,128)S(1)}, f32[8,1536]{1,0:T(8,128)S(1)}, u32[]{:S(2)}, u32[]{:S(2)}) collective-permute-start(f32[8,1536]{1,0:T(8,128)S(1)} %fusion), channel_id=1, source_target_pairs={{0,50},{1,51},{2,52},{3,53},{4,54},{5,55},{6,56},{7,57},{8,58},{9,... | collective-permute-start | bytes 147464
  1004.4 26.9 %collective-permute-start.52 = (f32[8,1536]{1,0:T(8,128)S(1)}, f32[8,1536]{1,0:T(8,128)S(1)}, u32[]{:S(2)}, u32[]{:S(2)}) collective-permute-start(f32[8,1536]{1,0:T(8,128)S(1)} %fusion), channel_id=1, source_target_pairs={{0,49},{1,50},{2,51},{3,52},{4,53},{5,54},{6,55},{7,56},{8,57},{9,... | collective-permute-start | bytes 147464
  1005.7 29.5 %collective-permute-start.51 = (f32[8,1536]{1,0:T(8,128)S(1)}, f32[8,1536]{1,0:T(8,128)S(1)}, u32[]{:S(2)}, u32[]{:S(2)}) collective-permute-start(f32[8,1536]{1,0:T(8,128)S(1)} %fusion), channel_id=1, source_target_pairs={{0,48},{1,49},{2,50},{3,51},{4,52},{5,53},{6,54},{7,55},{8,56},{9,... | collective-permute-start | bytes 147464
  1023.7 15.5 collective-permute-start.50
  1048.6 18.0 collective-permute-start.39
  1052.3 27.5 %collective-permute-start.38 = (f32[8,1536]{1,0:T(8,128)S(1)}, f32[8,1536]{1,0:T(8,128)S(1)}, u32[]{:S(2)}, u32[]{:S(2)}) collective-permute-start(f32[8,1536]{1,0:T(8,128)S(1)} %fusion), channel_id=1, source_target_pairs={{0,35},{1,36},{2,37},{3,38},{4,39},{5,40},{6,41},{7,42},{8,43},{9,... | collective-permute-start | bytes 147464
  1054.7 38.1 %collective-permute-start.37 = (f32[8,1536]{1,0:T(8,128)S(1)}, f32[8,1536]{1,0:T(8,128)S(1)}, u32[]{:S(2)}, u32[]{:S(2)}) collective-permute-start(f32[8,1536]{1,0:T(8,128)S(1)} %fusion), channel_id=1, source_target_pairs={{0,34},{1,35},{2,36},{3,37},{4,38},{5,39},{6,40},{7,41},{8,42},{9,... | collective-permute-start | bytes 147464
  1058.9 47.2 %collective-permute-start.36 = (f32[8,1536]{1,0:T(8,128)S(1)}, f32[8,1536]{1,0:T(8,128)S(1)}, u32[]{:S(2)}, u32[]{:S(2)}) collective-permute-start(f32[8,1536]{1,0:T(8,128)S(1)} %fusion), channel_id=1, source_target_pairs={{0,33},{1,34},{2,35},{3,36},{4,37},{5,38},{6,39},{7,40},{8,41},{9,... | collective-permute-start | bytes 147464
  1060.5 58.7 %collective-permute-start.35 = (f32[8,1536]{1,0:T(8,128)S(1)}, f32[8,1536]{1,0:T(8,128)S(1)}, u32[]{:S(2)}, u32[]{:S(2)}) collective-permute-start(f32[8,1536]{1,0:T(8,128)S(1)} %fusion), channel_id=1, source_target_pairs={{0,32},{1,33},{2,34},{3,35},{4,36},{5,37},{6,38},{7,39},{8,40},{9,... | collective-permute-start | bytes 147464
  1066.6 65.7 %collective-permute-start.34 = (f32[8,1536]{1,0:T(8,128)S(1)}, f32[8,1536]{1,0:T(8,128)S(1)}, u32[]{:S(2)}, u32[]{:S(2)}) collective-permute-start(f32[8,1536]{1,0:T(8,128)S(1)} %fusion), channel_id=1, source_target_pairs={{0,31},{1,32},{2,33},{3,34},{4,35},{5,36},{6,37},{7,38},{8,39},{9,... | collective-permute-start | bytes 147464
  1079.7 65.7 %collective-permute-start.33 = (f32[8,1536]{1,0:T(8,128)S(1)}, f32[8,1536]{1,0:T(8,128)S(1)}, u32[]{:S(2)}, u32[]{:S(2)}) collective-permute-start(f32[8,1536]{1,0:T(8,128)S(1)} %fusion), channel_id=1, source_target_pairs={{0,30},{1,31},{2,32},{3,33},{4,34},{5,35},{6,36},{7,37},{8,38},{9,... | collective-permute-start | bytes 147464
  1092.9 65.7 %collective-permute-start.32 = (f32[8,1536]{1,0:T(8,128)S(1)}, f32[8,1536]{1,0:T(8,128)S(1)}, u32[]{:S(2)}, u32[]{:S(2)}) collective-permute-start(f32[8,1536]{1,0:T(8,128)S(1)} %fusion), channel_id=1, source_target_pairs={{0,29},{1,30},{2,31},{3,32},{4,33},{5,34},{6,35},{7,36},{8,37},{9,... | collective-permute-start | bytes 147464
  1106.0 65.7 %collective-permute-start.31 = (f32[8,1536]{1,0:T(8,128)S(1)}, f32[8,1536]{1,0:T(8,128)S(1)}, u32[]{:S(2)}, u32[]{:S(2)}) collective-permute-start(f32[8,1536]{1,0:T(8,128)S(1)} %fusion), channel_id=1, source_target_pairs={{0,28},{1,29},{2,30},{3,31},{4,32},{5,33},{6,34},{7,35},{8,36},{9,... | collective-permute-start | bytes 147464
  1119.2 65.7 %collective-permute-start.30 = (f32[8,1536]{1,0:T(8,128)S(1)}, f32[8,1536]{1,0:T(8,128)S(1)}, u32[]{:S(2)}, u32[]{:S(2)}) collective-permute-start(f32[8,1536]{1,0:T(8,128)S(1)} %fusion), channel_id=1, source_target_pairs={{0,27},{1,28},{2,29},{3,30},{4,31},{5,32},{6,33},{7,34},{8,35},{9,... | collective-permute-start | bytes 147464
  1132.3 65.7 %collective-permute-start.29 = (f32[8,1536]{1,0:T(8,128)S(1)}, f32[8,1536]{1,0:T(8,128)S(1)}, u32[]{:S(2)}, u32[]{:S(2)}) collective-permute-start(f32[8,1536]{1,0:T(8,128)S(1)} %fusion), channel_id=1, source_target_pairs={{0,26},{1,27},{2,28},{3,29},{4,30},{5,31},{6,32},{7,33},{8,34},{9,... | collective-permute-start | bytes 147464
  1145.5 65.7 %collective-permute-start.28 = (f32[8,1536]{1,0:T(8,128)S(1)}, f32[8,1536]{1,0:T(8,128)S(1)}, u32[]{:S(2)}, u32[]{:S(2)}) collective-permute-start(f32[8,1536]{1,0:T(8,128)S(1)} %fusion), channel_id=1, source_target_pairs={{0,25},{1,26},{2,27},{3,28},{4,29},{5,30},{6,31},{7,32},{8,33},{9,... | collective-permute-start | bytes 147464
  1158.6 65.7 %collective-permute-start.27 = (f32[8,1536]{1,0:T(8,128)S(1)}, f32[8,1536]{1,0:T(8,128)S(1)}, u32[]{:S(2)}, u32[]{:S(2)}) collective-permute-start(f32[8,1536]{1,0:T(8,128)S(1)} %fusion), channel_id=1, source_target_pairs={{0,24},{1,25},{2,26},{3,27},{4,28},{5,29},{6,30},{7,31},{8,32},{9,... | collective-permute-start | bytes 147464
  1171.8 65.7 %collective-permute-start.26 = (f32[8,1536]{1,0:T(8,128)S(1)}, f32[8,1536]{1,0:T(8,128)S(1)}, u32[]{:S(2)}, u32[]{:S(2)}) collective-permute-start(f32[8,1536]{1,0:T(8,128)S(1)} %fusion), channel_id=1, source_target_pairs={{0,23},{1,24},{2,25},{3,26},{4,27},{5,28},{6,29},{7,30},{8,31},{9,... | collective-permute-start | bytes 147464
  1184.9 65.7 %collective-permute-start.25 = (f32[8,1536]{1,0:T(8,128)S(1)}, f32[8,1536]{1,0:T(8,128)S(1)}, u32[]{:S(2)}, u32[]{:S(2)}) collective-permute-start(f32[8,1536]{1,0:T(8,128)S(1)} %fusion), channel_id=1, source_target_pairs={{0,22},{1,23},{2,24},{3,25},{4,26},{5,27},{6,28},{7,29},{8,30},{9,... | collective-permute-start | bytes 147464
  1198.1 65.7 %collective-permute-start.24 = (f32[8,1536]{1,0:T(8,128)S(1)}, f32[8,1536]{1,0:T(8,128)S(1)}, u32[]{:S(2)}, u32[]{:S(2)}) collective-permute-start(f32[8,1536]{1,0:T(8,128)S(1)} %fusion), channel_id=1, source_target_pairs={{0,21},{1,22},{2,23},{3,24},{4,25},{5,26},{6,27},{7,28},{8,29},{9,... | collective-permute-start | bytes 147464
  1211.2 65.7 %collective-permute-start.23 = (f32[8,1536]{1,0:T(8,128)S(1)}, f32[8,1536]{1,0:T(8,128)S(1)}, u32[]{:S(2)}, u32[]{:S(2)}) collective-permute-start(f32[8,1536]{1,0:T(8,128)S(1)} %fusion), channel_id=1, source_target_pairs={{0,20},{1,21},{2,22},{3,23},{4,24},{5,25},{6,26},{7,27},{8,28},{9,... | collective-permute-start | bytes 147464
  1224.4 65.7 %collective-permute-start.22 = (f32[8,1536]{1,0:T(8,128)S(1)}, f32[8,1536]{1,0:T(8,128)S(1)}, u32[]{:S(2)}, u32[]{:S(2)}) collective-permute-start(f32[8,1536]{1,0:T(8,128)S(1)} %fusion), channel_id=1, source_target_pairs={{0,19},{1,20},{2,21},{3,22},{4,23},{5,24},{6,25},{7,26},{8,27},{9,... | collective-permute-start | bytes 147464
  1237.5 65.7 %collective-permute-start.21 = (f32[8,1536]{1,0:T(8,128)S(1)}, f32[8,1536]{1,0:T(8,128)S(1)}, u32[]{:S(2)}, u32[]{:S(2)}) collective-permute-start(f32[8,1536]{1,0:T(8,128)S(1)} %fusion), channel_id=1, source_target_pairs={{0,18},{1,19},{2,20},{3,21},{4,22},{5,23},{6,24},{7,25},{8,26},{9,... | collective-permute-start | bytes 147464
  1250.7 65.7 %collective-permute-start.20 = (f32[8,1536]{1,0:T(8,128)S(1)}, f32[8,1536]{1,0:T(8,128)S(1)}, u32[]{:S(2)}, u32[]{:S(2)}) collective-permute-start(f32[8,1536]{1,0:T(8,128)S(1)} %fusion), channel_id=1, source_target_pairs={{0,17},{1,18},{2,19},{3,20},{4,21},{5,22},{6,23},{7,24},{8,25},{9,... | collective-permute-start | bytes 147464
  1263.8 65.9 %collective-permute-start.19 = (f32[8,1536]{1,0:T(8,128)S(1)}, f32[8,1536]{1,0:T(8,128)S(1)}, u32[]{:S(2)}, u32[]{:S(2)}) collective-permute-start(f32[8,1536]{1,0:T(8,128)S(1)} %fusion), channel_id=1, source_target_pairs={{0,16},{1,17},{2,18},{3,19},{4,20},{5,21},{6,22},{7,23},{8,24},{9,... | collective-permute-start | bytes 147464
  1277.0 65.9 %collective-permute-start.18 = (f32[8,1536]{1,0:T(8,128)S(1)}, f32[8,1536]{1,0:T(8,128)S(1)}, u32[]{:S(2)}, u32[]{:S(2)}) collective-permute-start(f32[8,1536]{1,0:T(8,128)S(1)} %fusion), channel_id=1, source_target_pairs={{0,15},{1,16},{2,17},{3,18},{4,19},{5,20},{6,21},{7,22},{8,23},{9,... | collective-permute-start | bytes 147464
  1290.1 65.9 %collective-permute-start.17 = (f32[8,1536]{1,0:T(8,128)S(1)}, f32[8,1536]{1,0:T(8,128)S(1)}, u32[]{:S(2)}, u32[]{:S(2)}) collective-permute-start(f32[8,1536]{1,0:T(8,128)S(1)} %fusion), channel_id=1, source_target_pairs={{0,14},{1,15},{2,16},{3,17},{4,18},{5,19},{6,20},{7,21},{8,22},{9,... | collective-permute-start | bytes 147464
  1303.3 65.9 %collective-permute-start.16 = (f32[8,1536]{1,0:T(8,128)S(1)}, f32[8,1536]{1,0:T(8,128)S(1)}, u32[]{:S(2)}, u32[]{:S(2)}) collective-permute-start(f32[8,1536]{1,0:T(8,128)S(1)} %fusion), channel_id=1, source_target_pairs={{0,13},{1,14},{2,15},{3,16},{4,17},{5,18},{6,19},{7,20},{8,21},{9,... | collective-permute-start | bytes 147464
  1316.4 65.9 %collective-permute-start.15 = (f32[8,1536]{1,0:T(8,128)S(1)}, f32[8,1536]{1,0:T(8,128)S(1)}, u32[]{:S(2)}, u32[]{:S(2)}) collective-permute-start(f32[8,1536]{1,0:T(8,128)S(1)} %fusion), channel_id=1, source_target_pairs={{0,12},{1,13},{2,14},{3,15},{4,16},{5,17},{6,18},{7,19},{8,20},{9,... | collective-permute-start | bytes 147464
  1329.7 65.7 %collective-permute-start.14 = (f32[8,1536]{1,0:T(8,128)S(1)}, f32[8,1536]{1,0:T(8,128)S(1)}, u32[]{:S(2)}, u32[]{:S(2)}) collective-permute-start(f32[8,1536]{1,0:T(8,128)S(1)} %fusion), channel_id=1, source_target_pairs={{0,11},{1,12},{2,13},{3,14},{4,15},{5,16},{6,17},{7,18},{8,19},{9,... | collective-permute-start | bytes 147464
  1342.9 65.7 %collective-permute-start.13 = (f32[8,1536]{1,0:T(8,128)S(1)}, f32[8,1536]{1,0:T(8,128)S(1)}, u32[]{:S(2)}, u32[]{:S(2)}) collective-permute-start(f32[8,1536]{1,0:T(8,128)S(1)} %fusion), channel_id=1, source_target_pairs={{0,10},{1,11},{2,12},{3,13},{4,14},{5,15},{6,16},{7,17},{8,18},{9,... | collective-permute-start | bytes 147464
  1356.0 66.3 %collective-permute-start.12 = (f32[8,1536]{1,0:T(8,128)S(1)}, f32[8,1536]{1,0:T(8,128)S(1)}, u32[]{:S(2)}, u32[]{:S(2)}) collective-permute-start(f32[8,1536]{1,0:T(8,128)S(1)} %fusion), channel_id=1, source_target_pairs={{0,9},{1,10},{2,11},{3,12},{4,13},{5,14},{6,15},{7,16},{8,17},{9,1... | collective-permute-start | bytes 147464
  1369.2 66.3 %collective-permute-start.11 = (f32[8,1536]{1,0:T(8,128)S(1)}, f32[8,1536]{1,0:T(8,128)S(1)}, u32[]{:S(2)}, u32[]{:S(2)}) collective-permute-start(f32[8,1536]{1,0:T(8,128)S(1)} %fusion), channel_id=1, source_target_pairs={{0,8},{1,9},{2,10},{3,11},{4,12},{5,13},{6,14},{7,15},{8,16},{9,17... | collective-permute-start | bytes 147464
  1382.3 66.3 %collective-permute-start.10 = (f32[8,1536]{1,0:T(8,128)S(1)}, f32[8,1536]{1,0:T(8,128)S(1)}, u32[]{:S(2)}, u32[]{:S(2)}) collective-permute-start(f32[8,1536]{1,0:T(8,128)S(1)} %fusion), channel_id=1, source_target_pairs={{0,7},{1,8},{2,9},{3,10},{4,11},{5,12},{6,13},{7,14},{8,15},{9,16}... | collective-permute-start | bytes 147464
  1395.5 66.3 %collective-permute-start.9 = (f32[8,1536]{1,0:T(8,128)S(1)}, f32[8,1536]{1,0:T(8,128)S(1)}, u32[]{:S(2)}, u32[]{:S(2)}) collective-permute-start(f32[8,1536]{1,0:T(8,128)S(1)} %fusion), channel_id=1, source_target_pairs={{0,6},{1,7},{2,8},{3,9},{4,10},{5,11},{6,12},{7,13},{8,14},{9,15},... | collective-permute-start | bytes 147464
  1408.6 56.6 %collective-permute-start.8 = (f32[8,1536]{1,0:T(8,128)S(1)}, f32[8,1536]{1,0:T(8,128)}, u32[]{:S(2)}, u32[]{:S(2)}) collective-permute-start(f32[8,1536]{1,0:T(8,128)S(1)} %fusion), channel_id=1, source_target_pairs={{0,5},{1,6},{2,7},{3,8},{4,9},{5,10},{6,11},{7,12},{8,13},{9,14},{... | collective-permute-start | bytes 147464
  1422.4 42.8 %collective-permute-start.7 = (f32[8,1536]{1,0:T(8,128)S(1)}, f32[8,1536]{1,0:T(8,128)}, u32[]{:S(2)}, u32[]{:S(2)}) collective-permute-start(f32[8,1536]{1,0:T(8,128)S(1)} %fusion), channel_id=1, source_target_pairs={{0,4},{1,5},{2,6},{3,7},{4,8},{5,9},{6,10},{7,11},{8,12},{9,13},{1... | collective-permute-start | bytes 147464
  1435.5 29.7 %collective-permute-start.6 = (f32[8,1536]{1,0:T(8,128)S(1)}, f32[8,1536]{1,0:T(8,128)}, u32[]{:S(2)}, u32[]{:S(2)}) collective-permute-start(f32[8,1536]{1,0:T(8,128)S(1)} %fusion), channel_id=1, source_target_pairs={{0,3},{1,4},{2,5},{3,6},{4,7},{5,8},{6,9},{7,10},{8,11},{9,12},{10... | collective-permute-start | bytes 147464
  1448.7 16.5 collective-permute-start.5
  (110 other events, 11059.4 us)
Sparse Core Ops, SparseCore 0:
  11.9 120.5 all-gather.3
  1678.2 246.9 all-reduce.7
where the time goes:
time: 1950 us; the launch traced here: 1930 us
  blocking collectives  1010 us (52%)
  starting transfers between devices  502 us (26%)
  waiting for transfers between devices  239 us (12%)
  local copies, waits for them, and re-layouts  129 us (7%)
  other arithmetic  27.6 us (1%)
    unnamed x1, blocking collectives  710 us
    unnamed x65, starting transfers between devices  489 us
    unnamed x67, waiting for transfers between devices  239 us
    unnamed x183, local copies, waits for them, and re-layouts  109 us
    psum x1, blocking collectives, local(): lax.psum((jnp.sum(grad_pre * normed, axis=0), jnp.sum(grad_pre, axis=0)),...  79.5 us
    psum x1, blocking collectives, local(): lax.psum((jnp.sum(weight_col * conv, axis=0), jnp.sum(weight_col)), ('dp'...  75.7 us
    psum x1, blocking collectives, local(): lax.psum(jnp.sum(weight_col * centred * centred, axis=0), ('dp', 'pair'))  74.2 us
    all_gather x1, blocking collectives, local(): params_full = lax.all_gather(stacked, ('dp', 'pair'), axis=1, tiled=True)  68 us
  transfers between devices with their start and end apart: 70, of which 3 were waited for; matrix products, arithmetic and copies ran while one was open for 44% of the time, Pallas kernels for 0%

commit v1 on v0

--- a/solution.py
+++ b/solution.py
@@ -32,7 +32,10 @@
     device_pos = lax.axis_index(("dp", "pair"))
     weight_col = frame_mask.astype(jnp.float32)[:, None]
     stacked = jnp.concatenate([dw_kernel, norm_scale[None, :], norm_shift[None, :]], axis=0)
-    params_full = lax.all_gather(stacked, ("dp", "pair"), axis=1, tiled=True)
+    params_full = jnp.concatenate(
+        lax.all_to_all(jnp.stack([stacked] * lax.axis_size(("dp", "pair"))), ("dp", "pair"), 0, 0),
+        axis=1,
+    )
     kernel_full = params_full[:KERNEL]
     scale_full = params_full[KERNEL]
     shift_full = params_full[KERNEL + 1]

time: 1950 us -> 1920 us (0.985)
  blocking collectives: 1010 us -> 937 us
  local copies, waits for them, and re-layouts: 129 us -> 162 us
    all_gather x1 -> x0, blocking collectives: 68 us -> none  [local(): params_full = lax.all_gather(stacked, ('dp', 'pair'), axis=1, tiled=True)]
    mul x0 -> x32, local copies, waits for them, and re-layouts: none -> 21.7 us  [the longest x31 20.7 us: local(): kernel_full[offset] * padded_in[offset:offset + local_rows]]
    unnamed x183 -> x199, local copies, waits for them, and re-layouts: 109 us -> 111 us
  transfers between devices with their start and end apart: 70 -> 71, of which waited for: 3 -> 4; matrix products, arithmetic and copies ran while one was open for 44% -> 47% of each run, Pallas kernels for 0% -> 0%
where the time goes in v1:
time: 1920 us; the launch traced here: 1910 us
  blocking collectives  937 us (49%)
  starting transfers between devices  505 us (26%)
  waiting for transfers between devices  247 us (13%)
  local copies, waits for them, and re-layouts  162 us (8%)
  other arithmetic  34.3 us (2%)
    unnamed x1, blocking collectives  709 us
    unnamed x65, starting transfers between devices  478 us
    unnamed x67, waiting for transfers between devices  239 us
    unnamed x199, local copies, waits for them, and re-layouts  111 us
    psum x1, blocking collectives, local(): lax.psum((jnp.sum(grad_pre * normed, axis=0), jnp.sum(grad_pre, axis=0)),...  79.5 us
    psum x1, blocking collectives, local(): lax.psum(jnp.sum(weight_col * centred * centred, axis=0), ('dp', 'pair'))  74 us
    psum x1, blocking collectives, local(): lax.psum((jnp.sum(weight_col * conv, axis=0), jnp.sum(weight_col)), ('dp'...  73.7 us
  transfers between devices with their start and end apart: 71, of which 4 were waited for; matrix products, arithmetic and copies ran while one was open for 47% of the time, Pallas kernels for 0%

profile of v1, /device:TPU:1, one launch (start us, length us, event | category | flops | bytes accessed | tf_op | source)
XLA Modules:
  0.0 1914.8 jit_solution(2064241873499779715)
XLA Ops:
  9.7 4.6 collective-permute-start
  19.9 15.0 all-to-all-start
  41.6 8.8 all-to-all-done
  52.5 7.7 slice_reduce_fusion.31
  70.6 14.1 slice_reduce_fusion.32
  97.4 5.6 multiply_reduce_fusion.2
  103.1 73.7 %all-reduce.5 = (f32[1536]{0:T(1024)S(1)}, f32[]{:T(128)}) all-reduce(f32[1536]{0:T(1024)S(1)} %get-tuple-element.89, f32[]{:T(128)} %convert_reduce_fusion), channel_id=1, replica_groups=mesh['dp'=128,'pair'=2] {'dp','pair'}, use_global_device_ids=true, to_apply=%region_1.2 | all-reduce | flops 1537 | bytes 12296 | tf_op jit(solution)/shard_map/psum | solution.py:53
  177.6 74.0 %psum.37 = f32[1536]{0:T(1024)S(1)} all-reduce(f32[1536]{0:T(1024)S(1)} %fusion.119), channel_id=1, replica_groups=mesh['dp'=128,'pair'=2] {'dp','pair'}, use_global_device_ids=true, to_apply=%region_5.6 | all-reduce | flops 1536 | bytes 12288 | tf_op jit(solution)/shard_map/psum | solution.py:58
  252.3 5.2 fusion.124
  257.4 709.4 %fusion = f32[8,1536]{1,0:T(8,128)S(1)} fusion(f32[1536,1536]{1,0:T(8,128)} %fusion.124), kind=kCustom, calls=%all-reduce-scatter | all-reduce-scatter fusion | flops 3145729 | bytes 9486336
  971.7 11.0 collective-permute-start.67
  998.6 17.9 collective-permute-start.51
  1055.5 5.3 collective-permute-start.34
  1060.8 13.1 collective-permute-start.33
  1074.0 13.1 collective-permute-start.32
  1087.1 13.1 collective-permute-start.31
  1100.3 13.1 collective-permute-start.30
  1113.4 13.1 collective-permute-start.29
  1126.6 13.1 collective-permute-start.28
  1139.7 13.1 collective-permute-start.27
  1152.9 13.1 collective-permute-start.26
  1166.0 13.1 collective-permute-start.25
  1179.2 13.1 collective-permute-start.24
  1192.3 13.1 collective-permute-start.23
  1205.5 13.1 collective-permute-start.22
  1218.6 13.1 collective-permute-start.21
  1231.8 13.1 collective-permute-start.20
  1244.9 13.1 collective-permute-start.19
  1258.1 13.1 collective-permute-start.18
  1271.2 13.1 collective-permute-start.17
  1284.4 13.1 collective-permute-start.16
  1297.5 13.1 collective-permute-start.15
  1310.7 13.1 collective-permute-start.14
  1323.8 13.1 collective-permute-start.13
  1337.0 13.1 collective-permute-start.12
  1350.1 13.1 collective-permute-start.11
  1363.3 13.1 collective-permute-start.10
  1376.4 13.1 collective-permute-start.9
  1389.6 13.7 collective-permute-start.8
  1403.3 13.2 collective-permute-start.7
  1416.5 13.1 collective-permute-start.6
  1429.6 13.1 collective-permute-start.5
  1446.9 97.2 %concatenate.45 = f32[518,1536]{1,0:T(8,128)} concatenate(f32[6,1536]{1,0:T(8,128)S(1)} %collective-permute-done.67, f32[8,1536]{1,0:T(8,128)S(1)} %collective-permute-done.66, f32[8,1536]{1,0:T(8,128)S(1)} %collective-permute-done.65, f32[8,1536]{1,0:T(8,128)S(1)} %collective-permute-done.64, f32[8,1536]{1,0:T(8,128)S(1)} %collective-permute-done.63, ...), dimensions={0} | concatenate | bytes 6365184
  1545.6 8.4 reshape.124
  1554.0 4.1 convolution_convert_fusion
  1560.9 79.5 %all-reduce.4 = (f32[1536]{0:T(1024)S(1)}, f32[1536]{0:T(1024)S(1)}) all-reduce(f32[1536]{0:T(1024)S(1)} %get-tuple-element.83, f32[1536]{0:T(1024)S(1)} %get-tuple-element.82), channel_id=1, replica_groups=mesh['dp'=128,'pair'=2] {'dp','pair'}, use_global_device_ids=true, to_apply=%region_9.10 | all-reduce | flops 3072 | bytes 24576 | tf_op jit(solution)/shard_map/psum | solution.py:71
  1659.2 10.2 fusion.9
  1669.4 236.7 %all-reduce.8.cloned.1.call-done = f32[31,1536]{1,0:T(8,128)} async-done(((f32[31,1536]{1,0:T(8,128)}), f32[31,1536]{1,0:T(8,128)}) %all-reduce.8.cloned.1.call-update) | async-done | bytes 190480
  (399 shorter events, 127.7 us)
Async XLA Ops:
  7.2 1538.4 %all-gather.3.cloned.1.call-start = ((), (), s32[]{:S(2)}) async-start(), calls=%async_computation.1 | async-start | bytes 6316032 | tf_op jit(solution)/shard_map/all_gather | solution.py:65
  9.7 31.7 %collective-permute-start = (bf16[15,1536]{1,0:T(8,128)(2,1)S(1)}, bf16[15,1536]{1,0:T(8,128)(2,1)S(1)}, u32[]{:S(2)}, u32[]{:S(2)}) collective-permute-start(bf16[15,1536]{1,0:T(8,128)(2,1)S(1)} %get-tuple-element.93), channel_id=1, source_target_pairs={{0,1},{1,2},{2,3},{3,4},{4,5},{5,6},{6,7},{7,8},{8,9},{9,10},{10,1... | collective-permute-start | bytes 138248 | tf_op jit(solution)/shard_map/ppermute | solution.py:17
  14.3 27.1 %collective-permute-start.1 = (bf16[15,1536]{1,0:T(8,128)(2,1)S(1)}, bf16[15,1536]{1,0:T(8,128)(2,1)S(1)}, u32[]{:S(2)}, u32[]{:S(2)}) collective-permute-start(bf16[15,1536]{1,0:T(8,128)(2,1)S(1)} %get-tuple-element.94), channel_id=1, source_target_pairs={{1,0},{2,1},{3,2},{4,3},{5,4},{6,5},{7,6},{8,7},{9,8},{10,9},{11,1... | collective-permute-start | bytes 138248 | tf_op jit(solution)/shard_map/ppermute | solution.py:19
  19.9 30.5 %all-to-all-start = ((f32[256,1,198]{2,1,0:T(1,128)}), f32[256,1,198]{2,1,0:T(1,128)S(1)}, u32[]{:S(2)}, u32[]{:S(2)}) async-start(f32[256,1,198]{2,1,0:T(1,128)} %reshape.160), calls=%async_computation | async-start | bytes 524288 | tf_op jit(solution)/shard_map/all_to_all | solution.py:36
  35.0 1871.2 %all-reduce.8.cloned.1.call-start = ((), (), s32[]{:S(2)}) async-start(), calls=%async_computation.2 | async-start | bytes 393216
  966.9 18.7 collective-permute-start.66
  968.2 18.7 collective-permute-start.65
  970.4 17.8 collective-permute-start.64
  993.4 23.2 %collective-permute-start.55 = (f32[8,1536]{1,0:T(8,128)S(1)}, f32[8,1536]{1,0:T(8,128)S(1)}, u32[]{:S(2)}, u32[]{:S(2)}) collective-permute-start(f32[8,1536]{1,0:T(8,128)S(1)} %fusion), channel_id=1, source_target_pairs={{0,52},{1,53},{2,54},{3,55},{4,56},{5,57},{6,58},{7,59},{8,60},{9,... | collective-permute-start | bytes 147464
  994.7 25.0 %collective-permute-start.54 = (f32[8,1536]{1,0:T(8,128)S(1)}, f32[8,1536]{1,0:T(8,128)S(1)}, u32[]{:S(2)}, u32[]{:S(2)}) collective-permute-start(f32[8,1536]{1,0:T(8,128)S(1)} %fusion), channel_id=1, source_target_pairs={{0,51},{1,52},{2,53},{3,54},{4,55},{5,56},{6,57},{7,58},{8,59},{9,... | collective-permute-start | bytes 147464
  996.0 25.3 %collective-permute-start.53 = (f32[8,1536]{1,0:T(8,128)S(1)}, f32[8,1536]{1,0:T(8,128)S(1)}, u32[]{:S(2)}, u32[]{:S(2)}) collective-permute-start(f32[8,1536]{1,0:T(8,128)S(1)} %fusion), channel_id=1, source_target_pairs={{0,50},{1,51},{2,52},{3,53},{4,54},{5,55},{6,56},{7,57},{8,58},{9,... | collective-permute-start | bytes 147464
  997.3 26.9 %collective-permute-start.52 = (f32[8,1536]{1,0:T(8,128)S(1)}, f32[8,1536]{1,0:T(8,128)S(1)}, u32[]{:S(2)}, u32[]{:S(2)}) collective-permute-start(f32[8,1536]{1,0:T(8,128)S(1)} %fusion), channel_id=1, source_target_pairs={{0,49},{1,50},{2,51},{3,52},{4,53},{5,54},{6,55},{7,56},{8,57},{9,... | collective-permute-start | bytes 147464
  998.6 29.5 %collective-permute-start.51 = (f32[8,1536]{1,0:T(8,128)S(1)}, f32[8,1536]{1,0:T(8,128)S(1)}, u32[]{:S(2)}, u32[]{:S(2)}) collective-permute-start(f32[8,1536]{1,0:T(8,128)S(1)} %fusion), channel_id=1, source_target_pairs={{0,48},{1,49},{2,50},{3,51},{4,52},{5,53},{6,54},{7,55},{8,56},{9,... | collective-permute-start | bytes 147464
  1016.6 15.5 collective-permute-start.50
  1045.1 15.7 collective-permute-start.38
  1047.6 26.3 %collective-permute-start.37 = (f32[8,1536]{1,0:T(8,128)S(1)}, f32[8,1536]{1,0:T(8,128)S(1)}, u32[]{:S(2)}, u32[]{:S(2)}) collective-permute-start(f32[8,1536]{1,0:T(8,128)S(1)} %fusion), channel_id=1, source_target_pairs={{0,34},{1,35},{2,36},{3,37},{4,38},{5,39},{6,40},{7,41},{8,42},{9,... | collective-permute-start | bytes 147464
  1051.8 35.3 %collective-permute-start.36 = (f32[8,1536]{1,0:T(8,128)S(1)}, f32[8,1536]{1,0:T(8,128)S(1)}, u32[]{:S(2)}, u32[]{:S(2)}) collective-permute-start(f32[8,1536]{1,0:T(8,128)S(1)} %fusion), channel_id=1, source_target_pairs={{0,33},{1,34},{2,35},{3,36},{4,37},{5,38},{6,39},{7,40},{8,41},{9,... | collective-permute-start | bytes 147464
  1053.4 46.9 %collective-permute-start.35 = (f32[8,1536]{1,0:T(8,128)S(1)}, f32[8,1536]{1,0:T(8,128)S(1)}, u32[]{:S(2)}, u32[]{:S(2)}) collective-permute-start(f32[8,1536]{1,0:T(8,128)S(1)} %fusion), channel_id=1, source_target_pairs={{0,32},{1,33},{2,34},{3,35},{4,36},{5,37},{6,38},{7,39},{8,40},{9,... | collective-permute-start | bytes 147464
  1055.5 57.9 %collective-permute-start.34 = (f32[8,1536]{1,0:T(8,128)S(1)}, f32[8,1536]{1,0:T(8,128)S(1)}, u32[]{:S(2)}, u32[]{:S(2)}) collective-permute-start(f32[8,1536]{1,0:T(8,128)S(1)} %fusion), channel_id=1, source_target_pairs={{0,31},{1,32},{2,33},{3,34},{4,35},{5,36},{6,37},{7,38},{8,39},{9,... | collective-permute-start | bytes 147464
  1060.8 65.7 %collective-permute-start.33 = (f32[8,1536]{1,0:T(8,128)S(1)}, f32[8,1536]{1,0:T(8,128)S(1)}, u32[]{:S(2)}, u32[]{:S(2)}) collective-permute-start(f32[8,1536]{1,0:T(8,128)S(1)} %fusion), channel_id=1, source_target_pairs={{0,30},{1,31},{2,32},{3,33},{4,34},{5,35},{6,36},{7,37},{8,38},{9,... | collective-permute-start | bytes 147464
  1074.0 65.7 %collective-permute-start.32 = (f32[8,1536]{1,0:T(8,128)S(1)}, f32[8,1536]{1,0:T(8,128)S(1)}, u32[]{:S(2)}, u32[]{:S(2)}) collective-permute-start(f32[8,1536]{1,0:T(8,128)S(1)} %fusion), channel_id=1, source_target_pairs={{0,29},{1,30},{2,31},{3,32},{4,33},{5,34},{6,35},{7,36},{8,37},{9,... | collective-permute-start | bytes 147464
  1087.1 65.7 %collective-permute-start.31 = (f32[8,1536]{1,0:T(8,128)S(1)}, f32[8,1536]{1,0:T(8,128)S(1)}, u32[]{:S(2)}, u32[]{:S(2)}) collective-permute-start(f32[8,1536]{1,0:T(8,128)S(1)} %fusion), channel_id=1, source_target_pairs={{0,28},{1,29},{2,30},{3,31},{4,32},{5,33},{6,34},{7,35},{8,36},{9,... | collective-permute-start | bytes 147464
  1100.3 65.7 %collective-permute-start.30 = (f32[8,1536]{1,0:T(8,128)S(1)}, f32[8,1536]{1,0:T(8,128)S(1)}, u32[]{:S(2)}, u32[]{:S(2)}) collective-permute-start(f32[8,1536]{1,0:T(8,128)S(1)} %fusion), channel_id=1, source_target_pairs={{0,27},{1,28},{2,29},{3,30},{4,31},{5,32},{6,33},{7,34},{8,35},{9,... | collective-permute-start | bytes 147464
  1113.4 65.7 %collective-permute-start.29 = (f32[8,1536]{1,0:T(8,128)S(1)}, f32[8,1536]{1,0:T(8,128)S(1)}, u32[]{:S(2)}, u32[]{:S(2)}) collective-permute-start(f32[8,1536]{1,0:T(8,128)S(1)} %fusion), channel_id=1, source_target_pairs={{0,26},{1,27},{2,28},{3,29},{4,30},{5,31},{6,32},{7,33},{8,34},{9,... | collective-permute-start | bytes 147464
  1126.6 65.7 %collective-permute-start.28 = (f32[8,1536]{1,0:T(8,128)S(1)}, f32[8,1536]{1,0:T(8,128)S(1)}, u32[]{:S(2)}, u32[]{:S(2)}) collective-permute-start(f32[8,1536]{1,0:T(8,128)S(1)} %fusion), channel_id=1, source_target_pairs={{0,25},{1,26},{2,27},{3,28},{4,29},{5,30},{6,31},{7,32},{8,33},{9,... | collective-permute-start | bytes 147464
  1139.7 65.7 %collective-permute-start.27 = (f32[8,1536]{1,0:T(8,128)S(1)}, f32[8,1536]{1,0:T(8,128)S(1)}, u32[]{:S(2)}, u32[]{:S(2)}) collective-permute-start(f32[8,1536]{1,0:T(8,128)S(1)} %fusion), channel_id=1, source_target_pairs={{0,24},{1,25},{2,26},{3,27},{4,28},{5,29},{6,30},{7,31},{8,32},{9,... | collective-permute-start | bytes 147464
  1152.9 65.7 %collective-permute-start.26 = (f32[8,1536]{1,0:T(8,128)S(1)}, f32[8,1536]{1,0:T(8,128)S(1)}, u32[]{:S(2)}, u32[]{:S(2)}) collective-permute-start(f32[8,1536]{1,0:T(8,128)S(1)} %fusion), channel_id=1, source_target_pairs={{0,23},{1,24},{2,25},{3,26},{4,27},{5,28},{6,29},{7,30},{8,31},{9,... | collective-permute-start | bytes 147464
  1166.0 65.7 %collective-permute-start.25 = (f32[8,1536]{1,0:T(8,128)S(1)}, f32[8,1536]{1,0:T(8,128)S(1)}, u32[]{:S(2)}, u32[]{:S(2)}) collective-permute-start(f32[8,1536]{1,0:T(8,128)S(1)} %fusion), channel_id=1, source_target_pairs={{0,22},{1,23},{2,24},{3,25},{4,26},{5,27},{6,28},{7,29},{8,30},{9,... | collective-permute-start | bytes 147464
  1179.2 65.7 %collective-permute-start.24 = (f32[8,1536]{1,0:T(8,128)S(1)}, f32[8,1536]{1,0:T(8,128)S(1)}, u32[]{:S(2)}, u32[]{:S(2)}) collective-permute-start(f32[8,1536]{1,0:T(8,128)S(1)} %fusion), channel_id=1, source_target_pairs={{0,21},{1,22},{2,23},{3,24},{4,25},{5,26},{6,27},{7,28},{8,29},{9,... | collective-permute-start | bytes 147464
  1192.3 65.7 %collective-permute-start.23 = (f32[8,1536]{1,0:T(8,128)S(1)}, f32[8,1536]{1,0:T(8,128)S(1)}, u32[]{:S(2)}, u32[]{:S(2)}) collective-permute-start(f32[8,1536]{1,0:T(8,128)S(1)} %fusion), channel_id=1, source_target_pairs={{0,20},{1,21},{2,22},{3,23},{4,24},{5,25},{6,26},{7,27},{8,28},{9,... | collective-permute-start | bytes 147464
  1205.5 65.7 %collective-permute-start.22 = (f32[8,1536]{1,0:T(8,128)S(1)}, f32[8,1536]{1,0:T(8,128)S(1)}, u32[]{:S(2)}, u32[]{:S(2)}) collective-permute-start(f32[8,1536]{1,0:T(8,128)S(1)} %fusion), channel_id=1, source_target_pairs={{0,19},{1,20},{2,21},{3,22},{4,23},{5,24},{6,25},{7,26},{8,27},{9,... | collective-permute-start | bytes 147464
  1218.6 65.7 %collective-permute-start.21 = (f32[8,1536]{1,0:T(8,128)S(1)}, f32[8,1536]{1,0:T(8,128)S(1)}, u32[]{:S(2)}, u32[]{:S(2)}) collective-permute-start(f32[8,1536]{1,0:T(8,128)S(1)} %fusion), channel_id=1, source_target_pairs={{0,18},{1,19},{2,20},{3,21},{4,22},{5,23},{6,24},{7,25},{8,26},{9,... | collective-permute-start | bytes 147464
  1231.8 65.7 %collective-permute-start.20 = (f32[8,1536]{1,0:T(8,128)S(1)}, f32[8,1536]{1,0:T(8,128)S(1)}, u32[]{:S(2)}, u32[]{:S(2)}) collective-permute-start(f32[8,1536]{1,0:T(8,128)S(1)} %fusion), channel_id=1, source_target_pairs={{0,17},{1,18},{2,19},{3,20},{4,21},{5,22},{6,23},{7,24},{8,25},{9,... | collective-permute-start | bytes 147464
  1244.9 65.7 %collective-permute-start.19 = (f32[8,1536]{1,0:T(8,128)S(1)}, f32[8,1536]{1,0:T(8,128)S(1)}, u32[]{:S(2)}, u32[]{:S(2)}) collective-permute-start(f32[8,1536]{1,0:T(8,128)S(1)} %fusion), channel_id=1, source_target_pairs={{0,16},{1,17},{2,18},{3,19},{4,20},{5,21},{6,22},{7,23},{8,24},{9,... | collective-permute-start | bytes 147464
  1258.1 65.7 %collective-permute-start.18 = (f32[8,1536]{1,0:T(8,128)S(1)}, f32[8,1536]{1,0:T(8,128)S(1)}, u32[]{:S(2)}, u32[]{:S(2)}) collective-permute-start(f32[8,1536]{1,0:T(8,128)S(1)} %fusion), channel_id=1, source_target_pairs={{0,15},{1,16},{2,17},{3,18},{4,19},{5,20},{6,21},{7,22},{8,23},{9,... | collective-permute-start | bytes 147464
  1271.2 65.7 %collective-permute-start.17 = (f32[8,1536]{1,0:T(8,128)S(1)}, f32[8,1536]{1,0:T(8,128)S(1)}, u32[]{:S(2)}, u32[]{:S(2)}) collective-permute-start(f32[8,1536]{1,0:T(8,128)S(1)} %fusion), channel_id=1, source_target_pairs={{0,14},{1,15},{2,16},{3,17},{4,18},{5,19},{6,20},{7,21},{8,22},{9,... | collective-permute-start | bytes 147464
  1284.4 65.7 %collective-permute-start.16 = (f32[8,1536]{1,0:T(8,128)S(1)}, f32[8,1536]{1,0:T(8,128)S(1)}, u32[]{:S(2)}, u32[]{:S(2)}) collective-permute-start(f32[8,1536]{1,0:T(8,128)S(1)} %fusion), channel_id=1, source_target_pairs={{0,13},{1,14},{2,15},{3,16},{4,17},{5,18},{6,19},{7,20},{8,21},{9,... | collective-permute-start | bytes 147464
  1297.5 65.7 %collective-permute-start.15 = (f32[8,1536]{1,0:T(8,128)S(1)}, f32[8,1536]{1,0:T(8,128)S(1)}, u32[]{:S(2)}, u32[]{:S(2)}) collective-permute-start(f32[8,1536]{1,0:T(8,128)S(1)} %fusion), channel_id=1, source_target_pairs={{0,12},{1,13},{2,14},{3,15},{4,16},{5,17},{6,18},{7,19},{8,20},{9,... | collective-permute-start | bytes 147464
  1310.7 65.7 %collective-permute-start.14 = (f32[8,1536]{1,0:T(8,128)S(1)}, f32[8,1536]{1,0:T(8,128)S(1)}, u32[]{:S(2)}, u32[]{:S(2)}) collective-permute-start(f32[8,1536]{1,0:T(8,128)S(1)} %fusion), channel_id=1, source_target_pairs={{0,11},{1,12},{2,13},{3,14},{4,15},{5,16},{6,17},{7,18},{8,19},{9,... | collective-permute-start | bytes 147464
  1323.8 65.7 %collective-permute-start.13 = (f32[8,1536]{1,0:T(8,128)S(1)}, f32[8,1536]{1,0:T(8,128)S(1)}, u32[]{:S(2)}, u32[]{:S(2)}) collective-permute-start(f32[8,1536]{1,0:T(8,128)S(1)} %fusion), channel_id=1, source_target_pairs={{0,10},{1,11},{2,12},{3,13},{4,14},{5,15},{6,16},{7,17},{8,18},{9,... | collective-permute-start | bytes 147464
  1337.0 66.3 %collective-permute-start.12 = (f32[8,1536]{1,0:T(8,128)S(1)}, f32[8,1536]{1,0:T(8,128)S(1)}, u32[]{:S(2)}, u32[]{:S(2)}) collective-permute-start(f32[8,1536]{1,0:T(8,128)S(1)} %fusion), channel_id=1, source_target_pairs={{0,9},{1,10},{2,11},{3,12},{4,13},{5,14},{6,15},{7,16},{8,17},{9,1... | collective-permute-start | bytes 147464
  1350.1 66.3 %collective-permute-start.11 = (f32[8,1536]{1,0:T(8,128)S(1)}, f32[8,1536]{1,0:T(8,128)S(1)}, u32[]{:S(2)}, u32[]{:S(2)}) collective-permute-start(f32[8,1536]{1,0:T(8,128)S(1)} %fusion), channel_id=1, source_target_pairs={{0,8},{1,9},{2,10},{3,11},{4,12},{5,13},{6,14},{7,15},{8,16},{9,17... | collective-permute-start | bytes 147464
  1363.3 66.3 %collective-permute-start.10 = (f32[8,1536]{1,0:T(8,128)S(1)}, f32[8,1536]{1,0:T(8,128)S(1)}, u32[]{:S(2)}, u32[]{:S(2)}) collective-permute-start(f32[8,1536]{1,0:T(8,128)S(1)} %fusion), channel_id=1, source_target_pairs={{0,7},{1,8},{2,9},{3,10},{4,11},{5,12},{6,13},{7,14},{8,15},{9,16}... | collective-permute-start | bytes 147464
  1376.4 66.3 %collective-permute-start.9 = (f32[8,1536]{1,0:T(8,128)S(1)}, f32[8,1536]{1,0:T(8,128)S(1)}, u32[]{:S(2)}, u32[]{:S(2)}) collective-permute-start(f32[8,1536]{1,0:T(8,128)S(1)} %fusion), channel_id=1, source_target_pairs={{0,6},{1,7},{2,8},{3,9},{4,10},{5,11},{6,12},{7,13},{8,14},{9,15},... | collective-permute-start | bytes 147464
  1389.6 56.5 %collective-permute-start.8 = (f32[8,1536]{1,0:T(8,128)S(1)}, f32[8,1536]{1,0:T(8,128)}, u32[]{:S(2)}, u32[]{:S(2)}) collective-permute-start(f32[8,1536]{1,0:T(8,128)S(1)} %fusion), channel_id=1, source_target_pairs={{0,5},{1,6},{2,7},{3,8},{4,9},{5,10},{6,11},{7,12},{8,13},{9,14},{... | collective-permute-start | bytes 147464
  1403.3 42.8 %collective-permute-start.7 = (f32[8,1536]{1,0:T(8,128)S(1)}, f32[8,1536]{1,0:T(8,128)}, u32[]{:S(2)}, u32[]{:S(2)}) collective-permute-start(f32[8,1536]{1,0:T(8,128)S(1)} %fusion), channel_id=1, source_target_pairs={{0,4},{1,5},{2,6},{3,7},{4,8},{5,9},{6,10},{7,11},{8,12},{9,13},{1... | collective-permute-start | bytes 147464
  1416.5 29.7 %collective-permute-start.6 = (f32[8,1536]{1,0:T(8,128)S(1)}, f32[8,1536]{1,0:T(8,128)}, u32[]{:S(2)}, u32[]{:S(2)}) collective-permute-start(f32[8,1536]{1,0:T(8,128)S(1)} %fusion), channel_id=1, source_target_pairs={{0,3},{1,4},{2,5},{3,6},{4,7},{5,8},{6,9},{7,10},{8,11},{9,12},{10... | collective-permute-start | bytes 147464
  1429.6 16.5 collective-permute-start.5
  (118 other events, 10275.4 us)
Sparse Core Ops, SparseCore 0:
  11.9 121.0 all-gather.2
  1659.1 246.9 all-reduce.7
